TPU v7x, 32 devices: a whole 2x2x4 slice. The times are simulated.
32 devices in a mesh: variant: 4 (over y, x), sub: 8 (over z, core).
Axes of the slice: x: 2, y: 2, z: 4, core: 2. Of those that a mesh axis runs over, the one named last changes fastest.
Arguments:
- displacement: float32 [4, 6, 1024], P('variant', None, 'sub'), may hold values from -6 to 6
- neighbours: int32 [2, 1024], P(None, 'sub'), may hold values from 0 to 129, as said below
- micro_state: bfloat16 [4, 24576, 512], P('variant', 'sub'), may hold values from -6 to 6
- strain_loads: float32 [4, 6, 512], P('variant'), may hold values from -3 to 3
- stiffness: bfloat16 [4, 512, 512], P('variant'), may hold values from -0.25 to 0.25
- expand_weight: bfloat16 [4, 512, 2048], P('variant'), may hold values from -0.25 to 0.25
- contract_weight: bfloat16 [4, 2048, 512], P('variant'), may hold values from -0.125 to 0.125
- batch_route: int32 [4, 2, 192], P('variant', None, 'sub'), may hold values from -1 to 7, as said below
- yield_flags: int32 [4, 24576], P('variant', 'sub'), may hold values 0 or 1
- readout: bfloat16 [4, 512], P('variant'), may hold values from -0.75 to 0.75
- external_force: float32 [4, 1024], P('variant', 'sub'), may hold values from -6 to 6
- coarse_inverse: bfloat16 [4, 1024, 1024], P('variant', 'sub'), may hold values from -0.1875 to 0.1875
Outputs:
- states_next: bfloat16 [4, 24576, 512], P('variant', 'sub')
- coarse_correction: float32 [4, 1024], P('variant', 'sub')
Inputs may be any that keep to these rules, and one draw needn't show every extreme that they name: `neighbours`: entry 0 is position i or i + 1 of macro point i within its device (i counted from 0 in the device), entry 1 is i + 1 or i + 2, and entry 1 exceeds entry 0; the first and last point of each device use i and i + 2. `batch_route`: entry 0 of a batch held by device s on sub is -1 or (s + d) % 8 for some d from 1 to 4, each d used by at most one batch of s; entry 1 is -1 where entry 0 is, else its slot there, 0 to 1. Batches sent to one device have different slots; every device receives at most 2 batches, and in every draw some device receives 2.
All inputs are finite; a program needn't handle non-finite values. No bound on the sum of `yield_flags` on one device may be relied on, other than what follows from the above.
Results may differ from a plain program's by a relative error of at most 0.0055.
Values may be sent and summed in bfloat16 or wider, within the bound.
No kernel may reach another device: no remote copies, remote signals or barrier semaphores. Data moves between devices by JAX's collectives and lax.ppermute only.
A program may use at most 64 MiB of HBM per device.

v0:
```python
import functools

import jax
import jax.numpy as jnp
from jax import lax
from jax.experimental import pallas as pl
from jax.experimental.pallas import tpu as pltpu
from jax.sharding import PartitionSpec as P

BATCH = 128
GROUP = 16
TILE = 32
EDGE = 2
NEAR_CHIPS = 4
MIB = 1 << 20
F32 = jnp.float32
BF16 = jnp.bfloat16
NT = (((1,), (1,)), ((), ()))


def dot(a, b):
    return jnp.dot(a, b, preferred_element_type=F32)


def dot_nt(a, b, precision=None):
    return lax.dot_general(a, b, NT, precision=precision, preferred_element_type=F32)


def halves(x):
    high = x.astype(BF16)
    return high, (x - high.astype(F32)).astype(BF16)


def silu(a):
    half = 0.5 * a
    return half + half * jnp.tanh(half)


def list_alive(route_ref, list_ref, batches):
    count = jnp.int32(0)
    for b in range(batches):
        list_ref[count] = jnp.int32(b)
        count = count + (route_ref[0, 0, b] >= 0).astype(jnp.int32)
    return count


def stack_rows(ref):
    return jnp.concatenate([ref[k] for k in range(ref.shape[0])], axis=0)


def thirds(x):
    high = x.astype(BF16).astype(F32)
    middle = (x - high).astype(BF16).astype(F32)
    return high, middle, x - high - middle


def spread(strain, loads):
    blank = [jnp.zeros((GROUP - strain.shape[0] % GROUP, x.shape[1]), F32) for x in (strain, loads)]
    a, b, c = (jnp.concatenate([x, blank[0]], axis=0) for x in thirds(strain))
    d, e, f = (jnp.concatenate([x, blank[1]], axis=0) for x in thirds(loads))
    return lax.dot_general(
        jnp.concatenate([a, a, b, b, a, c], axis=0).astype(BF16),
        jnp.concatenate([d, e, d, e, f, d], axis=0).astype(BF16),
        (((0,), (0,)), ((), ())),
        preferred_element_type=F32,
    )


def strain_of(own, before, after, neighbours_ref):
    points = own.shape[1]
    place = lax.broadcasted_iota(jnp.int32, own.shape, 1)
    left = jnp.where(place == 0, before, pltpu.roll(own, 1, 1))
    right = jnp.where(place == points - 1, after, pltpu.roll(own, points - 1, 1))
    first, second = neighbours_ref[0:1, :], neighbours_ref[1:2, :]
    lower = jnp.where(first == place, left, own)
    upper = jnp.where(second == place + 2, right, own)
    return (upper - lower) / (second - first).astype(F32)


def elastic_kernel(
    per_point,
    blank_ref,
    field_ref,
    neighbours_ref,
    loads_ref,
    stiffness_ref,
    state_ref,
    elastic_ref,
    sum_ref,
    end_ref,
    mode_ref,
    point_ref,
):
    own = stack_rows(field_ref)
    points = own.shape[1]
    modes = state_ref.shape[2]
    tile = TILE * per_point
    strain = strain_of(own, blank_ref[...], blank_ref[...], neighbours_ref)
    loads = stack_rows(loads_ref)
    load = spread(strain, loads)
    loads = jnp.concatenate([loads, jnp.zeros((mode_ref.shape[0] - loads.shape[0], modes), F32)], axis=0)
    stiffness = stiffness_ref[0]
    high, low = halves(jnp.concatenate([load, loads], axis=0))
    shift = dot(high, stiffness) + dot(low, stiffness)
    point_ref[...] = shift[:points, :]
    mode_ref[...] = shift[points:, :]
    tiles = points // TILE
    edge = end_ref.shape[0] // 2
    for t in range(tiles):
        span, at = slice(t * tile, (t + 1) * tile), slice(t * TILE, (t + 1) * TILE)
        acc = dot(state_ref[0, span, :], stiffness)
        acc = acc.reshape(TILE, per_point, modes) + point_ref[at, :][:, None, :]
        elastic_ref[span, :] = acc.reshape(tile, modes).astype(BF16)
        sum_ref[at, :] = jnp.sum(acc, axis=1)
        if t == 0:
            end_ref[:edge, :] = acc.reshape(tile, modes)[:edge, :]
        if t == tiles - 1:
            end_ref[edge:, :] = acc.reshape(tile, modes)[tile - edge :, :]


def plastic_kernel(
    per_point,
    width,
    route_ref,
    core_ref,
    chip_ref,
    field_ref,
    neighbours_ref,
    expand_ref,
    contract_ref,
    flags_ref,
    readout_ref,
    force_ref,
    elastic_ref,
    start_ref,
    end_ref,
    mode_ref,
    out_ref,
    residual_ref,
    next_ref,
    list_ref,
    sum_ref,
    edge_ref,
    hidden_ref,
    bulk_sem,
    edge_sems,
):
    rows, modes = elastic_ref.shape
    points = rows // per_point
    batches = rows // BATCH
    edge = EDGE * per_point
    middle = slice(edge, rows - edge)
    bulk = pltpu.make_async_copy(elastic_ref.at[middle, :], out_ref.at[0, middle, :], bulk_sem)
    bulk.start()
    count = list_alive(route_ref, list_ref, batches)

    odd = lax.axis_index("sub") % 2 == 1
    own, core, chip = stack_rows(field_ref), stack_rows(core_ref), stack_rows(chip_ref)
    before = pltpu.roll(jnp.where(odd, core, chip), 1, 1)
    after = pltpu.roll(jnp.where(odd, chip, core), points - 1, 1)
    blank = jnp.zeros_like(own)
    change = strain_of(own, before, after, neighbours_ref) - strain_of(own, blank, blank, neighbours_ref)
    shifts = [
        jnp.sum(change[:, p : p + 1] * mode_ref[: own.shape[0], :], axis=0, keepdims=True)
        for p in (0, points - 1)
    ]
    ends = [slice(0, edge), slice(rows - edge, rows)]
    fixed = jnp.concatenate(
        [
            end_ref[:per_point, :] + shifts[0],
            end_ref[per_point : 2 * edge - per_point, :],
            end_ref[2 * edge - per_point :, :] + shifts[1],
        ],
        axis=0,
    ).astype(BF16)
    edge_ref[...] = fixed
    sum_ref[...] = start_ref[...]
    sum_ref[0:1, :] = start_ref[0:1, :] + per_point * shifts[0]
    sum_ref[points - 1 : points, :] = start_ref[points - 1 : points, :] + per_point * shifts[1]
    edges = [
        pltpu.make_async_copy(edge_ref.at[i * edge : (i + 1) * edge, :], out_ref.at[0, s, :], edge_sems.at[i])
        for i, s in enumerate(ends)
    ]
    for copy in edges:
        copy.start()

    def chunk(c):
        chosen = [list_ref[jnp.maximum(jnp.minimum(c * width + j, count - 1), 0)] for j in range(width)]
        starts = [pl.multiple_of(b * BATCH, BATCH) for b in chosen]
        parts = []
        for b, s in zip(chosen, starts):
            part = elastic_ref[pl.ds(s, BATCH), :]
            parts.append(jnp.where(b == 0, fixed[:edge, :], part[:edge, :]))
            parts.append(part[edge : BATCH - edge, :])
            parts.append(jnp.where(b == batches - 1, fixed[edge:, :], part[BATCH - edge :, :]))
        taken = jnp.concatenate(parts, axis=0)
        for h in range(0, expand_ref.shape[2], 512):
            hidden_ref[:, h : h + 512] = silu(dot(taken, expand_ref[0, :, h : h + 512])).astype(BF16)
        correction = dot(hidden_ref[...], contract_ref[0])
        p = lax.broadcasted_iota(jnp.int32, (points, BATCH), 0) * per_point
        r = lax.broadcasted_iota(jnp.int32, (points, BATCH), 1)
        owners, changes = [], []
        for j, s in enumerate(starts):
            at = slice(j * BATCH, (j + 1) * BATCH)
            flags = flags_ref[0:1, pl.ds(s, BATCH)].astype(F32)
            column = jnp.broadcast_to(flags, (BATCH, BATCH)).T
            column = jnp.concatenate([column] * (modes // BATCH), axis=1)
            change = column * correction[at, :]
            slot = pl.multiple_of((c * width + j) * BATCH, BATCH)
            next_ref[pl.ds(slot, BATCH), :] = (taken[at, :].astype(F32) + change).astype(BF16)
            row = r + jnp.where(c * width + j < count, s, -rows)
            owners.append(jnp.where((row >= p) & (row < p + per_point), 1.0, 0.0).astype(BF16))
            changes.append(change.astype(BF16))
        sum_ref[...] += dot(jnp.concatenate(owners, axis=1), jnp.concatenate(changes, axis=0))

    pl.loop(0, (count + width - 1) // width)(chunk)

    readout = jnp.broadcast_to(readout_ref[...].astype(F32), (GROUP, modes)).astype(BF16)
    parts = dot_nt(readout, jnp.concatenate(halves(sum_ref[...]), axis=0))[0:1, :]
    mean = (parts[:, :points] + parts[:, points:]) * (1.0 / per_point)
    residual_ref[...] = (force_ref[...] - mean).astype(BF16)
    for copy in [bulk] + edges:
        copy.wait()


def write_kernel(route_ref, next_ref, states_ref, out_ref, list_ref, sem):
    del states_ref
    count = list_alive(route_ref, list_ref, route_ref.shape[2])

    def changed(i):
        source = pl.ds(pl.multiple_of(i * BATCH, BATCH), BATCH)
        target = pl.ds(pl.multiple_of(list_ref[i] * BATCH, BATCH), BATCH)
        return pltpu.make_async_copy(next_ref.at[source, :], out_ref.at[0, target, :], sem)

    @pl.loop(0, count)
    def _(i):
        changed(i).start()

    @pl.loop(0, count)
    def _(i):
        changed(i).wait()


def blank_kernel(blank_ref):
    blank_ref[...] = jnp.zeros_like(blank_ref)


def coarse_kernel(inverse_ref, *refs):
    pairs, out_ref = refs[:-1], refs[-1]
    points = out_ref.shape[1]
    me = lax.axis_index("sub")
    values, columns = [], []
    for k, pair_ref in enumerate(pairs):
        chip = (me // 2) ^ k
        pair = pair_ref[...].astype(F32)
        for c in range(2):
            block = pl.multiple_of((2 * chip + (me + c) % 2) * points, points)
            values.append(jnp.broadcast_to(pair[c : c + 1, :], (GROUP, points)).astype(BF16))
            columns.append(inverse_ref[0, :, pl.ds(block, points)])
    total = dot_nt(jnp.concatenate(values, axis=1), jnp.concatenate(columns, axis=1))
    out_ref[...] = total[0:1, :]


def swap_pairs(n, offset):
    pairs = [(i, i + 1) for i in range(offset, n - 1, 2)]
    return pairs + [(j, i) for i, j in pairs]


def on_device(
    displacement,
    neighbours,
    micro_state,
    strain_loads,
    stiffness,
    expand_weight,
    contract_weight,
    batch_route,
    yield_flags,
    readout,
    external_force,
    coarse_inverse,
):
    n = lax.axis_size("sub")
    points = displacement.shape[2]
    rows, modes = micro_state.shape[1:]
    hidden_size = expand_weight.shape[2]
    per_point = rows // points
    batches = rows // BATCH
    reach = min(16, n // 2, batches)
    width = min(4, reach)
    slots = -(-reach // width) * width
    field = jnp.transpose(displacement, (1, 0, 2))
    loads = jnp.transpose(strain_loads, (1, 0, 2))
    vmem = pl.BlockSpec(memory_space=pltpu.VMEM)
    smem = pl.BlockSpec(memory_space=pltpu.SMEM)
    hbm = pl.BlockSpec(memory_space=pltpu.HBM)
    blank = pl.pallas_call(
        blank_kernel,
        out_shape=jax.ShapeDtypeStruct((displacement.shape[1], points), F32),
        out_specs=vmem,
        compiler_params=pltpu.CompilerParams(vmem_limit_bytes=MIB),
        cost_estimate=pl.CostEstimate(flops=20 * 10**9, bytes_accessed=MIB, transcendentals=0),
    )()
    from_core = lax.ppermute(field, "sub", swap_pairs(n, 0))
    from_chip = lax.ppermute(field, "sub", swap_pairs(n, 1))
    edge = EDGE * per_point
    kinds = -(-displacement.shape[1] // GROUP) * GROUP
    elastic, sums, ends, modes_out = pl.pallas_call(
        functools.partial(elastic_kernel, per_point),
        out_shape=(
            jax.ShapeDtypeStruct((rows, modes), BF16),
            jax.ShapeDtypeStruct((points, modes), F32),
            jax.ShapeDtypeStruct((2 * edge, modes), F32),
            jax.ShapeDtypeStruct((kinds, modes), F32),
        ),
        in_specs=[vmem] * 6,
        out_specs=(vmem,) * 4,
        scratch_shapes=[pltpu.VMEM((points, modes), F32)],
        compiler_params=pltpu.CompilerParams(vmem_limit_bytes=20 * MIB),
        cost_estimate=pl.CostEstimate(
            flops=2 * rows * modes * modes, bytes_accessed=8 * MIB, transcendentals=0
        ),
    )(blank, field, neighbours, loads, stiffness, micro_state)
    states, residual, updated = pl.pallas_call(
        functools.partial(plastic_kernel, per_point, width),
        out_shape=(
            jax.ShapeDtypeStruct((1, rows, modes), BF16),
            jax.ShapeDtypeStruct((1, points), BF16),
            jax.ShapeDtypeStruct((slots * BATCH, modes), BF16),
        ),
        in_specs=[smem] + [vmem] * 13,
        out_specs=(hbm, vmem, vmem),
        scratch_shapes=[
            pltpu.SMEM((batches + 1,), jnp.int32),
            pltpu.VMEM((points, modes), F32),
            pltpu.VMEM((2 * EDGE * per_point, modes), BF16),
            pltpu.VMEM((width * BATCH, hidden_size), BF16),
            pltpu.SemaphoreType.DMA(()),
            pltpu.SemaphoreType.DMA((2,)),
        ],
        compiler_params=pltpu.CompilerParams(vmem_limit_bytes=28 * MIB),
        cost_estimate=pl.CostEstimate(
            flops=4 * width * BATCH * modes * hidden_size, bytes_accessed=8 * MIB, transcendentals=0
        ),
    )(
        batch_route,
        from_core,
        from_chip,
        field,
        neighbours,
        expand_weight,
        contract_weight,
        yield_flags,
        readout,
        external_force,
        elastic,
        sums,
        ends,
        modes_out,
    )
    states_next = pl.pallas_call(
        write_kernel,
        out_shape=jax.ShapeDtypeStruct((1, rows, modes), BF16),
        in_specs=[smem, vmem, hbm],
        out_specs=hbm,
        scratch_shapes=[pltpu.SMEM((batches + 1,), jnp.int32), pltpu.SemaphoreType.DMA(())],
        input_output_aliases={2: 0},
        compiler_params=pltpu.CompilerParams(vmem_limit_bytes=4 * MIB),
        cost_estimate=pl.CostEstimate(flops=0, bytes_accessed=2 * MIB, transcendentals=0),
    )(batch_route, updated, states)
    if n // 2 > NEAR_CHIPS:
        everyone = lax.all_gather(residual, "sub", axis=1, tiled=True)[0]
        return states_next, dot(coarse_inverse[0], everyone)[None]
    other = lax.ppermute(residual, "sub", swap_pairs(n, 0))
    pair = jnp.concatenate([residual, other], axis=0)
    pairs = [pair] + [
        lax.ppermute(pair, "sub", [(i, i ^ (2 * k)) for i in range(n)]) for k in range(1, n // 2)
    ]
    coarse = pl.pallas_call(
        coarse_kernel,
        out_shape=jax.ShapeDtypeStruct((1, points), F32),
        in_specs=[vmem] * (1 + len(pairs)),
        out_specs=vmem,
        compiler_params=pltpu.CompilerParams(vmem_limit_bytes=4 * MIB),
    )(coarse_inverse, *pairs)
    return (states_next, coarse)


def solution(mesh):
    return jax.shard_map(
        on_device,
        mesh=mesh,
        in_specs=(
            P("variant", None, "sub"),
            P(None, "sub"),
            P("variant", "sub", None),
            P("variant", None, None),
            P("variant", None, None),
            P("variant", None, None),
            P("variant", None, None),
            P("variant", None, "sub"),
            P("variant", "sub"),
            P("variant", None),
            P("variant", "sub"),
            P("variant", "sub", None),
        ),
        out_specs=(P("variant", "sub", None), P("variant", "sub")),
        check_vma=False,
    )
```

profile of v0, /device:TPU:0, one launch (start us, length us, event | category | flops | bytes accessed | tf_op | source)
XLA Modules:
  0.0 21.5 jit_solution(12930194851138014881)
XLA Ops:
  0.6 0.0 copy-start.2
  0.6 0.0 copy-start.5
  0.7 0.0 copy-start.6
  0.7 0.0 copy-start.8
  0.7 0.0 copy-start.10
  0.7 0.8 %collective-permute-start.1 = (f32[6,1,128]{2,1,0:T(1,128)}, f32[6,1,128]{2,1,0:T(1,128)S(1)}, u32[]{:S(2)}, u32[]{:S(2)}) collective-permute-start(f32[6,1,128]{2,1,0:T(1,128)} %bitcast.3), channel_id=1, source_target_pairs={{1,2},{3,4},{5,6},{2,1},{4,3},{6,5},{9,10},{11,12},{13,14},{10,9},... | collective-permute-start | bytes 9224 | tf_op jit(solution)/shard_map/ppermute | solution.py:305
  1.5 4.6 %collective-permute-start = (f32[6,1,128]{2,1,0:T(1,128)}, f32[6,1,128]{2,1,0:T(1,128)S(1)}, u32[]{:S(2)}, u32[]{:S(2)}) collective-permute-start(f32[6,1,128]{2,1,0:T(1,128)} %bitcast.4), channel_id=1, source_target_pairs={{0,1},{2,3},{4,5},{6,7},{1,0},{3,2},{5,4},{7,6},{8,9},{10,11},{12,... | collective-permute-start | bytes 9224 | tf_op jit(solution)/shard_map/ppermute | solution.py:304
  6.1 0.0 copy-start.1
  6.1 0.0 copy-start.3
  6.1 0.0 copy-start.4
  6.1 0.0 copy-start.7
  6.1 0.0 copy-start.9
  6.1 0.0 copy-start.11
  6.1 0.0 copy-done.2
  6.1 0.0 copy-done.5
  6.1 0.0 copy-done.6
  6.1 0.0 copy-done.8
  6.2 0.0 copy-done.10
  6.2 2.3 %shard_map.132 = (bf16[3072,512]{1,0:T(8,128)(2,1)S(1)}, f32[128,512]{1,0:T(8,128)S(1)}, f32[96,512]{1,0:T(8,128)S(1)}, f32[16,512]{1,0:T(8,128)S(1)}) custom-call(f32[6,128]{1,0:T(8,128)S(1)} %shard_map.131.blank_ref, f32[6,1,128]{2,1,0:T(1,128)S(1)} %bitcast.5, s32[2,128]{1,0:T(2,128)S(1)} %copy-done.10, f32[6,1,512]{2,1,0:T(1,128)S(1)} %bitcast.2, ...), custom_call_target="tpu_custom_call" | custom-call | flops 1610612736 | bytes 8388608 | tf_op jit(solution)/shard_map/pallas_call | solution.py:308
  8.4 0.0 collective-permute-done.1.chip_ref
  8.4 0.0 collective-permute-done.core_ref
  8.4 0.0 copy-done.1
  8.5 0.0 copy-done.3
  8.5 0.0 copy-done.4
  8.5 0.0 copy-done.7
  8.5 0.0 copy-done.9
  8.5 0.0 copy-done.11
  8.5 2.3 %shard_map.133 = (bf16[1,3072,512]{2,1,0:T(8,128)(2,1)}, bf16[1,128]{1,0:T(2,128)(2,1)S(1)}, bf16[512,512]{1,0:T(8,128)(2,1)S(1)}) custom-call(s32[1,2,24]{2,1,0:T(2,128)S(1)} %copy-done.1, f32[6,1,128]{2,1,0:T(1,128)S(1)} %collective-permute-done.core_ref, f32[6,1,128]{2,1,0:T(1,128)S(1)} %collective-permute-done.1.chip_ref, f32[6,1,128]{2,1,0:T(1,128)S(1)} %bitcast.6, ...), custom_call_target="tpu_custom_call" | custom-call | flops 2147483648 | bytes 8388608 | tf_op jit(solution)/shard_map/pallas_call | solution.py:324
  10.8 0.1 collective-permute-start.2
  10.9 1.1 %collective-permute-done.2 = bf16[1,128]{1,0:T(2,128)(2,1)S(1)} collective-permute-done((bf16[1,128]{1,0:T(2,128)(2,1)S(1)}, bf16[1,128]{1,0:T(2,128)(2,1)S(1)}, u32[]{:S(2)}, u32[]{:S(2)}) %collective-permute-start.2) | collective-permute-done | bytes 288 | tf_op jit(solution)/shard_map/ppermute | solution.py:374
  12.0 4.3 %collective-permute-start.5 = (bf16[2,128]{1,0:T(2,128)(2,1)S(1)}, bf16[2,128]{1,0:T(2,128)(2,1)S(1)}, u32[]{:S(2)}, u32[]{:S(2)}) collective-permute-start(bf16[2,128]{1,0:T(2,128)(2,1)S(1)} %pad_maximum_fusion.refs_0_), channel_id=1, source_target_pairs={{0,6},{1,7},{2,4},{3,5},{4,2},{5,3},{6,0},{7,1},{8,14},{9,15},{10,... | collective-permute-start | bytes 1544 | tf_op jit(solution)/shard_map/ppermute | solution.py:377
  16.3 0.4 %collective-permute-start.4 = (bf16[2,128]{1,0:T(2,128)(2,1)S(1)}, bf16[2,128]{1,0:T(2,128)(2,1)S(1)}, u32[]{:S(2)}, u32[]{:S(2)}) collective-permute-start(bf16[2,128]{1,0:T(2,128)(2,1)S(1)} %pad_maximum_fusion.refs_0_), channel_id=1, source_target_pairs={{0,4},{1,5},{2,6},{3,7},{4,0},{5,1},{6,2},{7,3},{8,12},{9,13},{10,... | collective-permute-start | bytes 1544 | tf_op jit(solution)/shard_map/ppermute | solution.py:377
  16.7 0.3 %collective-permute-start.3 = (bf16[2,128]{1,0:T(2,128)(2,1)S(1)}, bf16[2,128]{1,0:T(2,128)(2,1)S(1)}, u32[]{:S(2)}, u32[]{:S(2)}) collective-permute-start(bf16[2,128]{1,0:T(2,128)(2,1)S(1)} %pad_maximum_fusion.refs_0_), channel_id=1, source_target_pairs={{0,2},{1,3},{2,0},{3,1},{4,6},{5,7},{6,4},{7,5},{8,10},{9,11},{10,... | collective-permute-start | bytes 1544 | tf_op jit(solution)/shard_map/ppermute | solution.py:377
  16.9 0.0 copy-start
  16.9 0.6 %shard_map.134 = bf16[1,3072,512]{2,1,0:T(8,128)(2,1)} custom-call(s32[1,2,24]{2,1,0:T(2,128)S(1)} %copy-done.1, bf16[512,512]{1,0:T(8,128)(2,1)S(1)} %get-tuple-element.13.next_ref, bf16[1,3072,512]{2,1,0:T(8,128)(2,1)} %get-tuple-element.14.states_ref), custom_call_target="tpu_custom_call", output_to_operand_aliasing={{}: (2, {})} | custom-call | bytes 2097152 | tf_op jit(solution)/shard_map/pallas_call | solution.py:361
  17.6 0.2 %collective-permute-done.5.refs_3_ = bf16[2,128]{1,0:T(2,128)(2,1)S(1)} collective-permute-done((bf16[2,128]{1,0:T(2,128)(2,1)S(1)}, bf16[2,128]{1,0:T(2,128)(2,1)S(1)}, u32[]{:S(2)}, u32[]{:S(2)}) %collective-permute-start.5) | collective-permute-done | bytes 544 | tf_op jit(solution)/shard_map/ppermute | solution.py:377
  17.8 2.9 %collective-permute-done.4.refs_2_ = bf16[2,128]{1,0:T(2,128)(2,1)S(1)} collective-permute-done((bf16[2,128]{1,0:T(2,128)(2,1)S(1)}, bf16[2,128]{1,0:T(2,128)(2,1)S(1)}, u32[]{:S(2)}, u32[]{:S(2)}) %collective-permute-start.4) | collective-permute-done | bytes 544 | tf_op jit(solution)/shard_map/ppermute | solution.py:377
  20.7 0.0 collective-permute-done.3.refs_1_
  20.7 0.0 copy-done
  20.7 0.7 %shard_map.135 = f32[1,128]{1,0:T(1,128)} custom-call(bf16[1,128,1024]{2,1,0:T(8,128)(2,1)S(1)} %copy-done, bf16[2,128]{1,0:T(2,128)(2,1)S(1)} %pad_maximum_fusion.refs_0_, bf16[2,128]{1,0:T(2,128)(2,1)S(1)} %collective-permute-done.3.refs_1_, bf16[2,128]{1,0:T(2,128)(2,1)S(1)} %collective-permute-done.4.refs_2_, ...), custom_call_target="tpu_custom_call" | custom-call | tf_op jit(solution)/shard_map/pallas_call | solution.py:379
  (2 shorter events, 0.0 us)
Async XLA Ops:
  0.6 5.5 %copy-start.2 = (bf16[1,3072,512]{2,1,0:T(8,128)(2,1)S(1)}, bf16[1,3072,512]{2,1,0:T(8,128)(2,1)}, u32[]{:S(2)}) copy-start(bf16[1,3072,512]{2,1,0:T(8,128)(2,1)} %state_ref.1) | copy-start | bytes 9437188
  0.6 5.5 %copy-start.5 = (bf16[1,512,512]{2,1,0:T(8,128)(2,1)S(1)}, bf16[1,512,512]{2,1,0:T(8,128)(2,1)}, u32[]{:S(2)}) copy-start(bf16[1,512,512]{2,1,0:T(8,128)(2,1)} %stiffness_ref.1) | copy-start | bytes 1572868
  0.7 5.5 %copy-start.6 = (f32[1,6,512]{2,0,1:T(1,128)S(1)}, f32[1,6,512]{2,0,1:T(1,128)}, u32[]{:S(2)}) copy-start(f32[1,6,512]{2,0,1:T(1,128)} %param.15) | copy-start | bytes 36868
  0.7 5.5 %copy-start.8 = (f32[1,6,128]{2,0,1:T(1,128)S(1)}, f32[1,6,128]{2,0,1:T(1,128)}, u32[]{:S(2)}) copy-start(f32[1,6,128]{2,0,1:T(1,128)} %param.12) | copy-start | bytes 9220
  0.7 5.5 %copy-start.10 = (s32[2,128]{1,0:T(2,128)S(1)}, s32[2,128]{1,0:T(2,128)}, u32[]{:S(2)}) copy-start(s32[2,128]{1,0:T(2,128)} %neighbours_ref.3) | copy-start | bytes 3076
  0.7 7.7 %collective-permute-start.1 = (f32[6,1,128]{2,1,0:T(1,128)}, f32[6,1,128]{2,1,0:T(1,128)S(1)}, u32[]{:S(2)}, u32[]{:S(2)}) collective-permute-start(f32[6,1,128]{2,1,0:T(1,128)} %bitcast.3), channel_id=1, source_target_pairs={{1,2},{3,4},{5,6},{2,1},{4,3},{6,5},{9,10},{11,12},{13,14},{10,9},... | collective-permute-start | bytes 9224 | tf_op jit(solution)/shard_map/ppermute | solution.py:305
  1.5 7.0 %collective-permute-start = (f32[6,1,128]{2,1,0:T(1,128)}, f32[6,1,128]{2,1,0:T(1,128)S(1)}, u32[]{:S(2)}, u32[]{:S(2)}) collective-permute-start(f32[6,1,128]{2,1,0:T(1,128)} %bitcast.4), channel_id=1, source_target_pairs={{0,1},{2,3},{4,5},{6,7},{1,0},{3,2},{5,4},{7,6},{8,9},{10,11},{12,... | collective-permute-start | bytes 9224 | tf_op jit(solution)/shard_map/ppermute | solution.py:304
  6.1 2.4 %copy-start.1 = (s32[1,2,24]{2,1,0:T(2,128)S(1)}, s32[1,2,24]{2,1,0:T(2,128)}, u32[]{:S(2)}) copy-start(s32[1,2,24]{2,1,0:T(2,128)} %route_ref.3) | copy-start | bytes 580
  6.1 2.4 %copy-start.3 = (bf16[1,512,2048]{2,1,0:T(8,128)(2,1)S(1)}, bf16[1,512,2048]{2,1,0:T(8,128)(2,1)}, u32[]{:S(2)}) copy-start(bf16[1,512,2048]{2,1,0:T(8,128)(2,1)} %expand_ref.1) | copy-start | bytes 6291460
  6.1 2.4 %copy-start.4 = (bf16[1,2048,512]{2,1,0:T(8,128)(2,1)S(1)}, bf16[1,2048,512]{2,1,0:T(8,128)(2,1)}, u32[]{:S(2)}) copy-start(bf16[1,2048,512]{2,1,0:T(8,128)(2,1)} %contract_ref.1) | copy-start | bytes 6291460
  6.1 2.4 %copy-start.7 = (s32[1,3072]{1,0:T(1,128)S(1)}, s32[1,3072]{1,0:T(1,128)}, u32[]{:S(2)}) copy-start(s32[1,3072]{1,0:T(1,128)} %flags_ref.1) | copy-start | bytes 36868
  6.1 2.4 %copy-start.9 = (bf16[1,512]{1,0:T(2,128)(2,1)S(1)}, bf16[1,512]{1,0:T(2,128)(2,1)}, u32[]{:S(2)}) copy-start(bf16[1,512]{1,0:T(2,128)(2,1)} %readout_ref.1) | copy-start | bytes 3076
  6.1 2.4 %copy-start.11 = (f32[1,128]{1,0:T(1,128)S(1)}, f32[1,128]{1,0:T(1,128)}, u32[]{:S(2)}) copy-start(f32[1,128]{1,0:T(1,128)} %force_ref.1) | copy-start | bytes 1540
  10.8 1.2 %collective-permute-start.2 = (bf16[1,128]{1,0:T(2,128)(2,1)S(1)}, bf16[1,128]{1,0:T(2,128)(2,1)S(1)}, u32[]{:S(2)}, u32[]{:S(2)}) collective-permute-start(bf16[1,128]{1,0:T(2,128)(2,1)S(1)} %get-tuple-element.15), channel_id=1, source_target_pairs={{0,1},{2,3},{4,5},{6,7},{1,0},{3,2},{5,4},{7,6},{8,9},{10,11},{12,... | collective-permute-start | bytes 776 | tf_op jit(solution)/shard_map/ppermute | solution.py:374
  12.0 5.8 %collective-permute-start.5 = (bf16[2,128]{1,0:T(2,128)(2,1)S(1)}, bf16[2,128]{1,0:T(2,128)(2,1)S(1)}, u32[]{:S(2)}, u32[]{:S(2)}) collective-permute-start(bf16[2,128]{1,0:T(2,128)(2,1)S(1)} %pad_maximum_fusion.refs_0_), channel_id=1, source_target_pairs={{0,6},{1,7},{2,4},{3,5},{4,2},{5,3},{6,0},{7,1},{8,14},{9,15},{10,... | collective-permute-start | bytes 1544 | tf_op jit(solution)/shard_map/ppermute | solution.py:377
  16.3 4.4 %collective-permute-start.4 = (bf16[2,128]{1,0:T(2,128)(2,1)S(1)}, bf16[2,128]{1,0:T(2,128)(2,1)S(1)}, u32[]{:S(2)}, u32[]{:S(2)}) collective-permute-start(bf16[2,128]{1,0:T(2,128)(2,1)S(1)} %pad_maximum_fusion.refs_0_), channel_id=1, source_target_pairs={{0,4},{1,5},{2,6},{3,7},{4,0},{5,1},{6,2},{7,3},{8,12},{9,13},{10,... | collective-permute-start | bytes 1544 | tf_op jit(solution)/shard_map/ppermute | solution.py:377
  16.7 4.1 %collective-permute-start.3 = (bf16[2,128]{1,0:T(2,128)(2,1)S(1)}, bf16[2,128]{1,0:T(2,128)(2,1)S(1)}, u32[]{:S(2)}, u32[]{:S(2)}) collective-permute-start(bf16[2,128]{1,0:T(2,128)(2,1)S(1)} %pad_maximum_fusion.refs_0_), channel_id=1, source_target_pairs={{0,2},{1,3},{2,0},{3,1},{4,6},{5,7},{6,4},{7,5},{8,10},{9,11},{10,... | collective-permute-start | bytes 1544 | tf_op jit(solution)/shard_map/ppermute | solution.py:377
  16.9 3.8 %copy-start = (bf16[1,128,1024]{2,1,0:T(8,128)(2,1)S(1)}, bf16[1,128,1024]{2,1,0:T(8,128)(2,1)}, u32[]{:S(2)}) copy-start(bf16[1,128,1024]{2,1,0:T(8,128)(2,1)} %inverse_ref.1) | copy-start | bytes 786436
where the time goes:
time: 21.2 us; the launch traced here: 21.5 us
  starting transfers between devices  10.4 us (49%)
  Pallas kernels  5.88 us (28%)
  waiting for transfers between devices  4.25 us (20%)
  between operations  0.84 us (4%)
    ppermute x3, starting transfers between devices, on_device(): lax.ppermute(pair, 'sub', [(i, i ^ 2 * k) for i in range(n)])  4.93 us
    ppermute x1, starting transfers between devices, on_device(): from_core = lax.ppermute(field, 'sub', swap_pairs(n, 0))  4.58 us
    ppermute x3, waiting for transfers between devices, on_device(): lax.ppermute(pair, 'sub', [(i, i ^ 2 * k) for i in range(n)])  3.17 us
    pallas_call x1, Pallas kernels, on_device(): pl.pallas_call(functools.partial(plastic_kernel, per_point, width), out_s...  2.3 us
    pallas_call x1, Pallas kernels, on_device(): pl.pallas_call(functools.partial(elastic_kernel, per_point), out_shape=(j...  2.25 us
    ppermute x1, waiting for transfers between devices, on_device(): other = lax.ppermute(residual, 'sub', swap_pairs(n, 0))  1.08 us
    ppermute x1, starting transfers between devices, on_device(): from_chip = lax.ppermute(field, 'sub', swap_pairs(n, 1))  0.79 us
    pallas_call x1, Pallas kernels, on_device(): pl.pallas_call(coarse_kernel, out_shape=jax.ShapeDtypeStruct((1, points),...  0.71 us
  transfers between devices with their start and end apart: 6, of which 3 were waited for; matrix products, arithmetic and copies ran while one was open for 0% of the time, Pallas kernels for 13%

commit v1 on v0

--- a/solution.py
+++ b/solution.py
@@ -139,7 +139,7 @@
     residual_ref,
     next_ref,
     list_ref,
-    sum_ref,
+    mean_ref,
     edge_ref,
     hidden_ref,
     bulk_sem,
@@ -174,9 +174,13 @@
         axis=0,
     ).astype(BF16)
     edge_ref[...] = fixed
-    sum_ref[...] = start_ref[...]
-    sum_ref[0:1, :] = start_ref[0:1, :] + per_point * shifts[0]
-    sum_ref[points - 1 : points, :] = start_ref[points - 1 : points, :] + per_point * shifts[1]
+    readout = jnp.broadcast_to(readout_ref[...].astype(F32), (GROUP, modes))
+    first, last = (jnp.sum(shift * readout[0:1, :], axis=1, keepdims=True) for shift in shifts)
+    readout = readout.astype(BF16)
+    base = dot_nt(readout, jnp.concatenate(halves(start_ref[...]), axis=0))[0:1, :]
+    place = lax.broadcasted_iota(jnp.int32, (1, points), 1)
+    moved = jnp.where(place == 0, first, 0.0) + jnp.where(place == points - 1, last, 0.0)
+    mean_ref[...] = moved + (base[:, :points] + base[:, points:]) * (1.0 / per_point)
     edges = [
         pltpu.make_async_copy(edge_ref.at[i * edge : (i + 1) * edge, :], out_ref.at[0, s, :], edge_sems.at[i])
         for i, s in enumerate(ends)
@@ -211,14 +215,13 @@
             row = r + jnp.where(c * width + j < count, s, -rows)
             owners.append(jnp.where((row >= p) & (row < p + per_point), 1.0, 0.0).astype(BF16))
             changes.append(change.astype(BF16))
-        sum_ref[...] += dot(jnp.concatenate(owners, axis=1), jnp.concatenate(changes, axis=0))
+        high, low = halves(dot_nt(readout, jnp.concatenate(changes, axis=0)))
+        share = dot_nt(jnp.concatenate([high, low], axis=0), jnp.concatenate(owners, axis=1))
+        mean_ref[...] += (share[0:1, :] + share[GROUP : GROUP + 1, :]) * (1.0 / per_point)
 
     pl.loop(0, (count + width - 1) // width)(chunk)
 
-    readout = jnp.broadcast_to(readout_ref[...].astype(F32), (GROUP, modes)).astype(BF16)
-    parts = dot_nt(readout, jnp.concatenate(halves(sum_ref[...]), axis=0))[0:1, :]
-    mean = (parts[:, :points] + parts[:, points:]) * (1.0 / per_point)
-    residual_ref[...] = (force_ref[...] - mean).astype(BF16)
+    residual_ref[...] = (force_ref[...] - mean_ref[...]).astype(BF16)
     for copy in [bulk] + edges:
         copy.wait()
 
@@ -332,7 +335,7 @@
         out_specs=(hbm, vmem, vmem),
         scratch_shapes=[
             pltpu.SMEM((batches + 1,), jnp.int32),
-            pltpu.VMEM((points, modes), F32),
+            pltpu.VMEM((1, points), F32),
             pltpu.VMEM((2 * EDGE * per_point, modes), BF16),
             pltpu.VMEM((width * BATCH, hidden_size), BF16),
             pltpu.SemaphoreType.DMA(()),

time: 21.2 us -> 21.5 us (1.014); the launches traced: 21.5 us -> 21.4 us
  waiting for transfers between devices: 4.25 us -> 3.22 us
  starting transfers between devices: 10.4 us -> 11.4 us
    ppermute x1, starting transfers between devices: 0.11 us -> 1.59 us  [on_device(): other = lax.ppermute(residual, 'sub', swap_pairs(n, 0))]
    ppermute x3, waiting for transfers between devices: 3.17 us -> 2.4 us  [on_device(): lax.ppermute(pair, 'sub', [(i, i ^ 2 * k) for i in range(n)])]
    ppermute x3, starting transfers between devices: 4.93 us -> 4.41 us  [on_device(): lax.ppermute(pair, 'sub', [(i, i ^ 2 * k) for i in range(n)])]
    ppermute x1, waiting for transfers between devices: 1.08 us -> 0.82 us  [on_device(): other = lax.ppermute(residual, 'sub', swap_pairs(n, 0))]
where the time goes in v1:
time: 21.5 us; the launch traced here: 21.4 us
  starting transfers between devices  11.4 us (53%)
  Pallas kernels  5.88 us (27%)
  waiting for transfers between devices  3.22 us (15%)
  between operations  0.84 us (4%)
    ppermute x1, starting transfers between devices, on_device(): from_core = lax.ppermute(field, 'sub', swap_pairs(n, 0))  4.58 us
    ppermute x3, starting transfers between devices, on_device(): lax.ppermute(pair, 'sub', [(i, i ^ 2 * k) for i in range(n)])  4.41 us
    ppermute x3, waiting for transfers between devices, on_device(): lax.ppermute(pair, 'sub', [(i, i ^ 2 * k) for i in range(n)])  2.4 us
    pallas_call x1, Pallas kernels, on_device(): pl.pallas_call(functools.partial(plastic_kernel, per_point, width), out_s...  2.29 us
    pallas_call x1, Pallas kernels, on_device(): pl.pallas_call(functools.partial(elastic_kernel, per_point), out_shape=(j...  2.25 us
    ppermute x1, starting transfers between devices, on_device(): other = lax.ppermute(residual, 'sub', swap_pairs(n, 0))  1.59 us
    ppermute x1, waiting for transfers between devices, on_device(): other = lax.ppermute(residual, 'sub', swap_pairs(n, 0))  0.82 us
    ppermute x1, starting transfers between devices, on_device(): from_chip = lax.ppermute(field, 'sub', swap_pairs(n, 1))  0.79 us
  transfers between devices with their start and end apart: 6, of which 3 were waited for; matrix products, arithmetic and copies ran while one was open for 0% of the time, Pallas kernels for 13%

profile of v1, /device:TPU:0, one launch (start us, length us, event | category | flops | bytes accessed | tf_op | source)
XLA Modules:
  0.0 21.4 jit_solution(8799490439807784663)
XLA Ops:
  0.6 0.0 copy-start.2
  0.6 0.0 copy-start.5
  0.7 0.0 copy-start.6
  0.7 0.0 copy-start.8
  0.7 0.0 copy-start.10
  0.7 0.8 %collective-permute-start.1 = (f32[6,1,128]{2,1,0:T(1,128)}, f32[6,1,128]{2,1,0:T(1,128)S(1)}, u32[]{:S(2)}, u32[]{:S(2)}) collective-permute-start(f32[6,1,128]{2,1,0:T(1,128)} %bitcast.3), channel_id=1, source_target_pairs={{1,2},{3,4},{5,6},{2,1},{4,3},{6,5},{9,10},{11,12},{13,14},{10,9},... | collective-permute-start | bytes 9224 | tf_op jit(solution)/shard_map/ppermute | solution.py:308
  1.5 4.6 %collective-permute-start = (f32[6,1,128]{2,1,0:T(1,128)}, f32[6,1,128]{2,1,0:T(1,128)S(1)}, u32[]{:S(2)}, u32[]{:S(2)}) collective-permute-start(f32[6,1,128]{2,1,0:T(1,128)} %bitcast.4), channel_id=1, source_target_pairs={{0,1},{2,3},{4,5},{6,7},{1,0},{3,2},{5,4},{7,6},{8,9},{10,11},{12,... | collective-permute-start | bytes 9224 | tf_op jit(solution)/shard_map/ppermute | solution.py:307
  6.1 0.0 copy-start.1
  6.1 0.0 copy-start.3
  6.1 0.0 copy-start.4
  6.1 0.0 copy-start.7
  6.1 0.0 copy-start.9
  6.1 0.0 copy-start.11
  6.1 0.0 copy-done.2
  6.1 0.0 copy-done.5
  6.1 0.0 copy-done.6
  6.1 0.0 copy-done.8
  6.2 0.0 copy-done.10
  6.2 2.3 %shard_map.132 = (bf16[3072,512]{1,0:T(8,128)(2,1)S(1)}, f32[128,512]{1,0:T(8,128)S(1)}, f32[96,512]{1,0:T(8,128)S(1)}, f32[16,512]{1,0:T(8,128)S(1)}) custom-call(f32[6,128]{1,0:T(8,128)S(1)} %shard_map.131.blank_ref, f32[6,1,128]{2,1,0:T(1,128)S(1)} %bitcast.5, s32[2,128]{1,0:T(2,128)S(1)} %copy-done.10, f32[6,1,512]{2,1,0:T(1,128)S(1)} %bitcast.2, ...), custom_call_target="tpu_custom_call" | custom-call | flops 1610612736 | bytes 8388608 | tf_op jit(solution)/shard_map/pallas_call | solution.py:311
  8.4 0.0 collective-permute-done.1.chip_ref
  8.4 0.0 collective-permute-done.core_ref
  8.4 0.0 copy-done.1
  8.5 0.0 copy-done.3
  8.5 0.0 copy-done.4
  8.5 0.0 copy-done.7
  8.5 0.0 copy-done.9
  8.5 0.0 copy-done.11
  8.5 2.3 %shard_map.133 = (bf16[1,3072,512]{2,1,0:T(8,128)(2,1)}, bf16[1,128]{1,0:T(2,128)(2,1)S(1)}, bf16[512,512]{1,0:T(8,128)(2,1)S(1)}) custom-call(s32[1,2,24]{2,1,0:T(2,128)S(1)} %copy-done.1, f32[6,1,128]{2,1,0:T(1,128)S(1)} %collective-permute-done.core_ref, f32[6,1,128]{2,1,0:T(1,128)S(1)} %collective-permute-done.1.chip_ref, f32[6,1,128]{2,1,0:T(1,128)S(1)} %bitcast.6, ...), custom_call_target="tpu_custom_call" | custom-call | flops 2147483648 | bytes 8388608 | tf_op jit(solution)/shard_map/pallas_call | solution.py:327
  10.8 1.6 %collective-permute-start.2 = (bf16[1,128]{1,0:T(2,128)(2,1)S(1)}, bf16[1,128]{1,0:T(2,128)(2,1)S(1)}, u32[]{:S(2)}, u32[]{:S(2)}) collective-permute-start(bf16[1,128]{1,0:T(2,128)(2,1)S(1)} %get-tuple-element.15), channel_id=1, source_target_pairs={{0,1},{2,3},{4,5},{6,7},{1,0},{3,2},{5,4},{7,6},{8,9},{10,11},{12,... | collective-permute-start | bytes 776 | tf_op jit(solution)/shard_map/ppermute | solution.py:377
  12.4 0.8 %collective-permute-done.2 = bf16[1,128]{1,0:T(2,128)(2,1)S(1)} collective-permute-done((bf16[1,128]{1,0:T(2,128)(2,1)S(1)}, bf16[1,128]{1,0:T(2,128)(2,1)S(1)}, u32[]{:S(2)}, u32[]{:S(2)}) %collective-permute-start.2) | collective-permute-done | bytes 288 | tf_op jit(solution)/shard_map/ppermute | solution.py:377
  13.2 3.0 %collective-permute-start.5 = (bf16[2,128]{1,0:T(2,128)(2,1)S(1)}, bf16[2,128]{1,0:T(2,128)(2,1)S(1)}, u32[]{:S(2)}, u32[]{:S(2)}) collective-permute-start(bf16[2,128]{1,0:T(2,128)(2,1)S(1)} %pad_maximum_fusion.refs_0_), channel_id=1, source_target_pairs={{0,6},{1,7},{2,4},{3,5},{4,2},{5,3},{6,0},{7,1},{8,14},{9,15},{10,... | collective-permute-start | bytes 1544 | tf_op jit(solution)/shard_map/ppermute | solution.py:380
  16.2 0.4 %collective-permute-start.4 = (bf16[2,128]{1,0:T(2,128)(2,1)S(1)}, bf16[2,128]{1,0:T(2,128)(2,1)S(1)}, u32[]{:S(2)}, u32[]{:S(2)}) collective-permute-start(bf16[2,128]{1,0:T(2,128)(2,1)S(1)} %pad_maximum_fusion.refs_0_), channel_id=1, source_target_pairs={{0,4},{1,5},{2,6},{3,7},{4,0},{5,1},{6,2},{7,3},{8,12},{9,13},{10,... | collective-permute-start | bytes 1544 | tf_op jit(solution)/shard_map/ppermute | solution.py:380
  16.6 1.0 %collective-permute-start.3 = (bf16[2,128]{1,0:T(2,128)(2,1)S(1)}, bf16[2,128]{1,0:T(2,128)(2,1)S(1)}, u32[]{:S(2)}, u32[]{:S(2)}) collective-permute-start(bf16[2,128]{1,0:T(2,128)(2,1)S(1)} %pad_maximum_fusion.refs_0_), channel_id=1, source_target_pairs={{0,2},{1,3},{2,0},{3,1},{4,6},{5,7},{6,4},{7,5},{8,10},{9,11},{10,... | collective-permute-start | bytes 1544 | tf_op jit(solution)/shard_map/ppermute | solution.py:380
  17.6 0.0 copy-start
  17.6 0.6 %shard_map.134 = bf16[1,3072,512]{2,1,0:T(8,128)(2,1)} custom-call(s32[1,2,24]{2,1,0:T(2,128)S(1)} %copy-done.1, bf16[512,512]{1,0:T(8,128)(2,1)S(1)} %get-tuple-element.13.next_ref, bf16[1,3072,512]{2,1,0:T(8,128)(2,1)} %get-tuple-element.14.states_ref), custom_call_target="tpu_custom_call", output_to_operand_aliasing={{}: (2, {})} | custom-call | bytes 2097152 | tf_op jit(solution)/shard_map/pallas_call | solution.py:364
  18.3 0.3 %collective-permute-done.5.refs_3_ = bf16[2,128]{1,0:T(2,128)(2,1)S(1)} collective-permute-done((bf16[2,128]{1,0:T(2,128)(2,1)S(1)}, bf16[2,128]{1,0:T(2,128)(2,1)S(1)}, u32[]{:S(2)}, u32[]{:S(2)}) %collective-permute-start.5) | collective-permute-done | bytes 544 | tf_op jit(solution)/shard_map/ppermute | solution.py:380
  18.6 2.1 %collective-permute-done.4.refs_2_ = bf16[2,128]{1,0:T(2,128)(2,1)S(1)} collective-permute-done((bf16[2,128]{1,0:T(2,128)(2,1)S(1)}, bf16[2,128]{1,0:T(2,128)(2,1)S(1)}, u32[]{:S(2)}, u32[]{:S(2)}) %collective-permute-start.4) | collective-permute-done | bytes 544 | tf_op jit(solution)/shard_map/ppermute | solution.py:380
  20.7 0.0 collective-permute-done.3.refs_1_
  20.7 0.0 copy-done
  20.7 0.7 %shard_map.135 = f32[1,128]{1,0:T(1,128)} custom-call(bf16[1,128,1024]{2,1,0:T(8,128)(2,1)S(1)} %copy-done, bf16[2,128]{1,0:T(2,128)(2,1)S(1)} %pad_maximum_fusion.refs_0_, bf16[2,128]{1,0:T(2,128)(2,1)S(1)} %collective-permute-done.3.refs_1_, bf16[2,128]{1,0:T(2,128)(2,1)S(1)} %collective-permute-done.4.refs_2_, ...), custom_call_target="tpu_custom_call" | custom-call | tf_op jit(solution)/shard_map/pallas_call | solution.py:382
  (2 shorter events, 0.0 us)
Async XLA Ops:
  0.6 5.5 %copy-start.2 = (bf16[1,3072,512]{2,1,0:T(8,128)(2,1)S(1)}, bf16[1,3072,512]{2,1,0:T(8,128)(2,1)}, u32[]{:S(2)}) copy-start(bf16[1,3072,512]{2,1,0:T(8,128)(2,1)} %state_ref.1) | copy-start | bytes 9437188
  0.6 5.5 %copy-start.5 = (bf16[1,512,512]{2,1,0:T(8,128)(2,1)S(1)}, bf16[1,512,512]{2,1,0:T(8,128)(2,1)}, u32[]{:S(2)}) copy-start(bf16[1,512,512]{2,1,0:T(8,128)(2,1)} %stiffness_ref.1) | copy-start | bytes 1572868
  0.7 5.5 %copy-start.6 = (f32[1,6,512]{2,0,1:T(1,128)S(1)}, f32[1,6,512]{2,0,1:T(1,128)}, u32[]{:S(2)}) copy-start(f32[1,6,512]{2,0,1:T(1,128)} %param.15) | copy-start | bytes 36868
  0.7 5.5 %copy-start.8 = (f32[1,6,128]{2,0,1:T(1,128)S(1)}, f32[1,6,128]{2,0,1:T(1,128)}, u32[]{:S(2)}) copy-start(f32[1,6,128]{2,0,1:T(1,128)} %param.12) | copy-start | bytes 9220
  0.7 5.5 %copy-start.10 = (s32[2,128]{1,0:T(2,128)S(1)}, s32[2,128]{1,0:T(2,128)}, u32[]{:S(2)}) copy-start(s32[2,128]{1,0:T(2,128)} %neighbours_ref.3) | copy-start | bytes 3076
  0.7 7.7 %collective-permute-start.1 = (f32[6,1,128]{2,1,0:T(1,128)}, f32[6,1,128]{2,1,0:T(1,128)S(1)}, u32[]{:S(2)}, u32[]{:S(2)}) collective-permute-start(f32[6,1,128]{2,1,0:T(1,128)} %bitcast.3), channel_id=1, source_target_pairs={{1,2},{3,4},{5,6},{2,1},{4,3},{6,5},{9,10},{11,12},{13,14},{10,9},... | collective-permute-start | bytes 9224 | tf_op jit(solution)/shard_map/ppermute | solution.py:308
  1.5 7.0 %collective-permute-start = (f32[6,1,128]{2,1,0:T(1,128)}, f32[6,1,128]{2,1,0:T(1,128)S(1)}, u32[]{:S(2)}, u32[]{:S(2)}) collective-permute-start(f32[6,1,128]{2,1,0:T(1,128)} %bitcast.4), channel_id=1, source_target_pairs={{0,1},{2,3},{4,5},{6,7},{1,0},{3,2},{5,4},{7,6},{8,9},{10,11},{12,... | collective-permute-start | bytes 9224 | tf_op jit(solution)/shard_map/ppermute | solution.py:307
  6.1 2.4 %copy-start.1 = (s32[1,2,24]{2,1,0:T(2,128)S(1)}, s32[1,2,24]{2,1,0:T(2,128)}, u32[]{:S(2)}) copy-start(s32[1,2,24]{2,1,0:T(2,128)} %route_ref.3) | copy-start | bytes 580
  6.1 2.4 %copy-start.3 = (bf16[1,512,2048]{2,1,0:T(8,128)(2,1)S(1)}, bf16[1,512,2048]{2,1,0:T(8,128)(2,1)}, u32[]{:S(2)}) copy-start(bf16[1,512,2048]{2,1,0:T(8,128)(2,1)} %expand_ref.1) | copy-start | bytes 6291460
  6.1 2.4 %copy-start.4 = (bf16[1,2048,512]{2,1,0:T(8,128)(2,1)S(1)}, bf16[1,2048,512]{2,1,0:T(8,128)(2,1)}, u32[]{:S(2)}) copy-start(bf16[1,2048,512]{2,1,0:T(8,128)(2,1)} %contract_ref.1) | copy-start | bytes 6291460
  6.1 2.4 %copy-start.7 = (s32[1,3072]{1,0:T(1,128)S(1)}, s32[1,3072]{1,0:T(1,128)}, u32[]{:S(2)}) copy-start(s32[1,3072]{1,0:T(1,128)} %flags_ref.1) | copy-start | bytes 36868
  6.1 2.4 %copy-start.9 = (bf16[1,512]{1,0:T(2,128)(2,1)S(1)}, bf16[1,512]{1,0:T(2,128)(2,1)}, u32[]{:S(2)}) copy-start(bf16[1,512]{1,0:T(2,128)(2,1)} %readout_ref.1) | copy-start | bytes 3076
  6.1 2.4 %copy-start.11 = (f32[1,128]{1,0:T(1,128)S(1)}, f32[1,128]{1,0:T(1,128)}, u32[]{:S(2)}) copy-start(f32[1,128]{1,0:T(1,128)} %force_ref.1) | copy-start | bytes 1540
  10.8 2.4 %collective-permute-start.2 = (bf16[1,128]{1,0:T(2,128)(2,1)S(1)}, bf16[1,128]{1,0:T(2,128)(2,1)S(1)}, u32[]{:S(2)}, u32[]{:S(2)}) collective-permute-start(bf16[1,128]{1,0:T(2,128)(2,1)S(1)} %get-tuple-element.15), channel_id=1, source_target_pairs={{0,1},{2,3},{4,5},{6,7},{1,0},{3,2},{5,4},{7,6},{8,9},{10,11},{12,... | collective-permute-start | bytes 776 | tf_op jit(solution)/shard_map/ppermute | solution.py:377
  13.2 5.4 %collective-permute-start.5 = (bf16[2,128]{1,0:T(2,128)(2,1)S(1)}, bf16[2,128]{1,0:T(2,128)(2,1)S(1)}, u32[]{:S(2)}, u32[]{:S(2)}) collective-permute-start(bf16[2,128]{1,0:T(2,128)(2,1)S(1)} %pad_maximum_fusion.refs_0_), channel_id=1, source_target_pairs={{0,6},{1,7},{2,4},{3,5},{4,2},{5,3},{6,0},{7,1},{8,14},{9,15},{10,... | collective-permute-start | bytes 1544 | tf_op jit(solution)/shard_map/ppermute | solution.py:380
  16.2 4.4 %collective-permute-start.4 = (bf16[2,128]{1,0:T(2,128)(2,1)S(1)}, bf16[2,128]{1,0:T(2,128)(2,1)S(1)}, u32[]{:S(2)}, u32[]{:S(2)}) collective-permute-start(bf16[2,128]{1,0:T(2,128)(2,1)S(1)} %pad_maximum_fusion.refs_0_), channel_id=1, source_target_pairs={{0,4},{1,5},{2,6},{3,7},{4,0},{5,1},{6,2},{7,3},{8,12},{9,13},{10,... | collective-permute-start | bytes 1544 | tf_op jit(solution)/shard_map/ppermute | solution.py:380
  16.6 4.1 %collective-permute-start.3 = (bf16[2,128]{1,0:T(2,128)(2,1)S(1)}, bf16[2,128]{1,0:T(2,128)(2,1)S(1)}, u32[]{:S(2)}, u32[]{:S(2)}) collective-permute-start(bf16[2,128]{1,0:T(2,128)(2,1)S(1)} %pad_maximum_fusion.refs_0_), channel_id=1, source_target_pairs={{0,2},{1,3},{2,0},{3,1},{4,6},{5,7},{6,4},{7,5},{8,10},{9,11},{10,... | collective-permute-start | bytes 1544 | tf_op jit(solution)/shard_map/ppermute | solution.py:380
  17.6 3.0 %copy-start = (bf16[1,128,1024]{2,1,0:T(8,128)(2,1)S(1)}, bf16[1,128,1024]{2,1,0:T(8,128)(2,1)}, u32[]{:S(2)}) copy-start(bf16[1,128,1024]{2,1,0:T(8,128)(2,1)} %inverse_ref.1) | copy-start | bytes 786436

commit v2 on v1

--- a/solution.py
+++ b/solution.py
@@ -122,8 +122,8 @@
     per_point,
     width,
     route_ref,
+    chip_ref,
     core_ref,
-    chip_ref,
     field_ref,
     neighbours_ref,
     expand_ref,
@@ -347,8 +347,8 @@
         ),
     )(
         batch_route,
+        from_chip,
         from_core,
-        from_chip,
         field,
         neighbours,
         expand_weight,

time: 21.5 us -> 21.2 us (0.986); the launches traced: 21.4 us -> 21.5 us
  starting transfers between devices: 11.4 us -> 10.1 us
  waiting for transfers between devices: 3.22 us -> 3.99 us
  local copies, waits for them, and re-layouts: 0.05 us -> 0.61 us
    ppermute x1, starting transfers between devices: 4.58 us -> 0.52 us  [on_device(): from_core = lax.ppermute(field, 'sub', swap_pairs(n, 0))]
    ppermute x1, starting transfers between devices: 1.59 us -> 3.65 us  [on_device(): other = lax.ppermute(residual, 'sub', swap_pairs(n, 0))]
    ppermute x3, starting transfers between devices: 4.41 us -> 5.2 us  [on_device(): lax.ppermute(pair, 'sub', [(i, i ^ 2 * k) for i in range(n)])]
    ppermute x3, waiting for transfers between devices: 2.4 us -> 3.17 us  [on_device(): lax.ppermute(pair, 'sub', [(i, i ^ 2 * k) for i in range(n)])]
    unnamed x24, local copies, waits for them, and re-layouts: 0.05 us -> 0.61 us
where the time goes in v2:
time: 21.2 us; the launch traced here: 21.5 us
  starting transfers between devices  10.1 us (48%)
  Pallas kernels  5.87 us (28%)
  waiting for transfers between devices  3.99 us (19%)
  between operations  0.83 us (4%)
  local copies, waits for them, and re-layouts  0.61 us (3%)
    ppermute x3, starting transfers between devices, on_device(): lax.ppermute(pair, 'sub', [(i, i ^ 2 * k) for i in range(n)])  5.2 us
    ppermute x1, starting transfers between devices, on_device(): other = lax.ppermute(residual, 'sub', swap_pairs(n, 0))  3.65 us
    ppermute x3, waiting for transfers between devices, on_device(): lax.ppermute(pair, 'sub', [(i, i ^ 2 * k) for i in range(n)])  3.17 us
    pallas_call x1, Pallas kernels, on_device(): pl.pallas_call(functools.partial(plastic_kernel, per_point, width), out_s...  2.29 us
    pallas_call x1, Pallas kernels, on_device(): pl.pallas_call(functools.partial(elastic_kernel, per_point), out_shape=(j...  2.24 us
    ppermute x1, waiting for transfers between devices, on_device(): other = lax.ppermute(residual, 'sub', swap_pairs(n, 0))  0.82 us
    ppermute x1, starting transfers between devices, on_device(): from_chip = lax.ppermute(field, 'sub', swap_pairs(n, 1))  0.78 us
    pallas_call x1, Pallas kernels, on_device(): pl.pallas_call(coarse_kernel, out_shape=jax.ShapeDtypeStruct((1, points),...  0.71 us
  transfers between devices with their start and end apart: 6, of which 3 were waited for; matrix products, arithmetic and copies ran while one was open for 0% of the time, Pallas kernels for 13%

profile of v2, /device:TPU:0, one launch (start us, length us, event | category | flops | bytes accessed | tf_op | source)
XLA Modules:
  0.0 21.5 jit_solution(11947856723867492859)
XLA Ops:
  0.6 0.0 copy-start.2
  0.6 0.0 copy-start.5
  0.7 0.0 copy-start.6
  0.7 0.0 copy-start.8
  0.7 0.0 copy-start.10
  0.7 0.5 %collective-permute-start.1 = (f32[6,1,128]{2,1,0:T(1,128)}, f32[6,1,128]{2,1,0:T(1,128)S(1)}, u32[]{:S(2)}, u32[]{:S(2)}) collective-permute-start(f32[6,1,128]{2,1,0:T(1,128)} %bitcast.3), channel_id=1, source_target_pairs={{0,1},{2,3},{4,5},{6,7},{1,0},{3,2},{5,4},{7,6},{8,9},{10,11},{12,... | collective-permute-start | bytes 9224 | tf_op jit(solution)/shard_map/ppermute | solution.py:307
  1.2 0.8 %collective-permute-start = (f32[6,1,128]{2,1,0:T(1,128)}, f32[6,1,128]{2,1,0:T(1,128)S(1)}, u32[]{:S(2)}, u32[]{:S(2)}) collective-permute-start(f32[6,1,128]{2,1,0:T(1,128)} %bitcast.4), channel_id=1, source_target_pairs={{1,2},{3,4},{5,6},{2,1},{4,3},{6,5},{9,10},{11,12},{13,14},{10,9},... | collective-permute-start | bytes 9224 | tf_op jit(solution)/shard_map/ppermute | solution.py:308
  2.0 0.0 copy-start.1
  2.0 0.0 copy-start.3
  2.0 0.0 copy-start.4
  2.0 0.0 copy-start.7
  2.0 0.0 copy-start.9
  2.1 0.0 copy-start.11
  2.1 0.5 %copy-done.2 = bf16[1,3072,512]{2,1,0:T(8,128)(2,1)S(1)} copy-done((bf16[1,3072,512]{2,1,0:T(8,128)(2,1)S(1)}, bf16[1,3072,512]{2,1,0:T(8,128)(2,1)}, u32[]{:S(2)}) %copy-start.2) | copy-done | bytes 3145752
  2.5 0.1 copy-done.5
  2.6 0.0 copy-done.6
  2.6 0.0 copy-done.8
  2.6 0.0 copy-done.10
  2.6 2.2 %shard_map.132 = (bf16[3072,512]{1,0:T(8,128)(2,1)S(1)}, f32[128,512]{1,0:T(8,128)S(1)}, f32[96,512]{1,0:T(8,128)S(1)}, f32[16,512]{1,0:T(8,128)S(1)}) custom-call(f32[6,128]{1,0:T(8,128)S(1)} %shard_map.131.blank_ref, f32[6,1,128]{2,1,0:T(1,128)S(1)} %bitcast.5, s32[2,128]{1,0:T(2,128)S(1)} %copy-done.10, f32[6,1,512]{2,1,0:T(1,128)S(1)} %bitcast.2, ...), custom_call_target="tpu_custom_call" | custom-call | flops 1610612736 | bytes 8388608 | tf_op jit(solution)/shard_map/pallas_call | solution.py:311
  4.9 0.0 collective-permute-done.1.core_ref
  4.9 0.0 collective-permute-done.chip_ref
  4.9 0.0 copy-done.1
  4.9 0.0 copy-done.3
  4.9 0.0 copy-done.4
  4.9 0.0 copy-done.7
  4.9 0.0 copy-done.9
  5.0 0.0 copy-done.11
  5.0 2.3 %shard_map.133 = (bf16[1,3072,512]{2,1,0:T(8,128)(2,1)}, bf16[1,128]{1,0:T(2,128)(2,1)S(1)}, bf16[512,512]{1,0:T(8,128)(2,1)S(1)}) custom-call(s32[1,2,24]{2,1,0:T(2,128)S(1)} %copy-done.1, f32[6,1,128]{2,1,0:T(1,128)S(1)} %collective-permute-done.chip_ref, f32[6,1,128]{2,1,0:T(1,128)S(1)} %collective-permute-done.1.core_ref, f32[6,1,128]{2,1,0:T(1,128)S(1)} %bitcast.6, ...), custom_call_target="tpu_custom_call" | custom-call | flops 2147483648 | bytes 8388608 | tf_op jit(solution)/shard_map/pallas_call | solution.py:327
  7.3 3.6 %collective-permute-start.2 = (bf16[1,128]{1,0:T(2,128)(2,1)S(1)}, bf16[1,128]{1,0:T(2,128)(2,1)S(1)}, u32[]{:S(2)}, u32[]{:S(2)}) collective-permute-start(bf16[1,128]{1,0:T(2,128)(2,1)S(1)} %get-tuple-element.15), channel_id=1, source_target_pairs={{0,1},{2,3},{4,5},{6,7},{1,0},{3,2},{5,4},{7,6},{8,9},{10,11},{12,... | collective-permute-start | bytes 776 | tf_op jit(solution)/shard_map/ppermute | solution.py:377
  10.9 0.8 %collective-permute-done.2 = bf16[1,128]{1,0:T(2,128)(2,1)S(1)} collective-permute-done((bf16[1,128]{1,0:T(2,128)(2,1)S(1)}, bf16[1,128]{1,0:T(2,128)(2,1)S(1)}, u32[]{:S(2)}, u32[]{:S(2)}) %collective-permute-start.2) | collective-permute-done | bytes 288 | tf_op jit(solution)/shard_map/ppermute | solution.py:377
  11.7 4.6 %collective-permute-start.5 = (bf16[2,128]{1,0:T(2,128)(2,1)S(1)}, bf16[2,128]{1,0:T(2,128)(2,1)S(1)}, u32[]{:S(2)}, u32[]{:S(2)}) collective-permute-start(bf16[2,128]{1,0:T(2,128)(2,1)S(1)} %pad_maximum_fusion.refs_0_), channel_id=1, source_target_pairs={{0,6},{1,7},{2,4},{3,5},{4,2},{5,3},{6,0},{7,1},{8,14},{9,15},{10,... | collective-permute-start | bytes 1544 | tf_op jit(solution)/shard_map/ppermute | solution.py:380
  16.3 0.0 collective-permute-start.4
  16.3 0.6 %collective-permute-start.3 = (bf16[2,128]{1,0:T(2,128)(2,1)S(1)}, bf16[2,128]{1,0:T(2,128)(2,1)S(1)}, u32[]{:S(2)}, u32[]{:S(2)}) collective-permute-start(bf16[2,128]{1,0:T(2,128)(2,1)S(1)} %pad_maximum_fusion.refs_0_), channel_id=1, source_target_pairs={{0,2},{1,3},{2,0},{3,1},{4,6},{5,7},{6,4},{7,5},{8,10},{9,11},{10,... | collective-permute-start | bytes 1544 | tf_op jit(solution)/shard_map/ppermute | solution.py:380
  16.9 0.0 copy-start
  16.9 0.6 %shard_map.134 = bf16[1,3072,512]{2,1,0:T(8,128)(2,1)} custom-call(s32[1,2,24]{2,1,0:T(2,128)S(1)} %copy-done.1, bf16[512,512]{1,0:T(8,128)(2,1)S(1)} %get-tuple-element.13.next_ref, bf16[1,3072,512]{2,1,0:T(8,128)(2,1)} %get-tuple-element.14.states_ref), custom_call_target="tpu_custom_call", output_to_operand_aliasing={{}: (2, {})} | custom-call | bytes 2097152 | tf_op jit(solution)/shard_map/pallas_call | solution.py:364
  17.6 0.3 %collective-permute-done.5.refs_3_ = bf16[2,128]{1,0:T(2,128)(2,1)S(1)} collective-permute-done((bf16[2,128]{1,0:T(2,128)(2,1)S(1)}, bf16[2,128]{1,0:T(2,128)(2,1)S(1)}, u32[]{:S(2)}, u32[]{:S(2)}) %collective-permute-start.5) | collective-permute-done | bytes 544 | tf_op jit(solution)/shard_map/ppermute | solution.py:380
  17.8 2.9 %collective-permute-done.4.refs_2_ = bf16[2,128]{1,0:T(2,128)(2,1)S(1)} collective-permute-done((bf16[2,128]{1,0:T(2,128)(2,1)S(1)}, bf16[2,128]{1,0:T(2,128)(2,1)S(1)}, u32[]{:S(2)}, u32[]{:S(2)}) %collective-permute-start.4) | collective-permute-done | bytes 544 | tf_op jit(solution)/shard_map/ppermute | solution.py:380
  20.7 0.0 collective-permute-done.3.refs_1_
  20.7 0.0 copy-done
  20.7 0.7 %shard_map.135 = f32[1,128]{1,0:T(1,128)} custom-call(bf16[1,128,1024]{2,1,0:T(8,128)(2,1)S(1)} %copy-done, bf16[2,128]{1,0:T(2,128)(2,1)S(1)} %pad_maximum_fusion.refs_0_, bf16[2,128]{1,0:T(2,128)(2,1)S(1)} %collective-permute-done.3.refs_1_, bf16[2,128]{1,0:T(2,128)(2,1)S(1)} %collective-permute-done.4.refs_2_, ...), custom_call_target="tpu_custom_call" | custom-call | tf_op jit(solution)/shard_map/pallas_call | solution.py:382
  (2 shorter events, 0.0 us)
Async XLA Ops:
  0.6 1.9 %copy-start.2 = (bf16[1,3072,512]{2,1,0:T(8,128)(2,1)S(1)}, bf16[1,3072,512]{2,1,0:T(8,128)(2,1)}, u32[]{:S(2)}) copy-start(bf16[1,3072,512]{2,1,0:T(8,128)(2,1)} %state_ref.1) | copy-start | bytes 9437188
  0.6 2.0 %copy-start.5 = (bf16[1,512,512]{2,1,0:T(8,128)(2,1)S(1)}, bf16[1,512,512]{2,1,0:T(8,128)(2,1)}, u32[]{:S(2)}) copy-start(bf16[1,512,512]{2,1,0:T(8,128)(2,1)} %stiffness_ref.1) | copy-start | bytes 1572868
  0.7 2.0 %copy-start.6 = (f32[1,6,512]{2,0,1:T(1,128)S(1)}, f32[1,6,512]{2,0,1:T(1,128)}, u32[]{:S(2)}) copy-start(f32[1,6,512]{2,0,1:T(1,128)} %param.15) | copy-start | bytes 36868
  0.7 2.0 %copy-start.8 = (f32[1,6,128]{2,0,1:T(1,128)S(1)}, f32[1,6,128]{2,0,1:T(1,128)}, u32[]{:S(2)}) copy-start(f32[1,6,128]{2,0,1:T(1,128)} %param.12) | copy-start | bytes 9220
  0.7 2.0 %copy-start.10 = (s32[2,128]{1,0:T(2,128)S(1)}, s32[2,128]{1,0:T(2,128)}, u32[]{:S(2)}) copy-start(s32[2,128]{1,0:T(2,128)} %neighbours_ref.3) | copy-start | bytes 3076
  0.7 4.2 %collective-permute-start.1 = (f32[6,1,128]{2,1,0:T(1,128)}, f32[6,1,128]{2,1,0:T(1,128)S(1)}, u32[]{:S(2)}, u32[]{:S(2)}) collective-permute-start(f32[6,1,128]{2,1,0:T(1,128)} %bitcast.3), channel_id=1, source_target_pairs={{0,1},{2,3},{4,5},{6,7},{1,0},{3,2},{5,4},{7,6},{8,9},{10,11},{12,... | collective-permute-start | bytes 9224 | tf_op jit(solution)/shard_map/ppermute | solution.py:307
  1.2 3.7 %collective-permute-start = (f32[6,1,128]{2,1,0:T(1,128)}, f32[6,1,128]{2,1,0:T(1,128)S(1)}, u32[]{:S(2)}, u32[]{:S(2)}) collective-permute-start(f32[6,1,128]{2,1,0:T(1,128)} %bitcast.4), channel_id=1, source_target_pairs={{1,2},{3,4},{5,6},{2,1},{4,3},{6,5},{9,10},{11,12},{13,14},{10,9},... | collective-permute-start | bytes 9224 | tf_op jit(solution)/shard_map/ppermute | solution.py:308
  2.0 2.9 %copy-start.1 = (s32[1,2,24]{2,1,0:T(2,128)S(1)}, s32[1,2,24]{2,1,0:T(2,128)}, u32[]{:S(2)}) copy-start(s32[1,2,24]{2,1,0:T(2,128)} %route_ref.3) | copy-start | bytes 580
  2.0 2.9 %copy-start.3 = (bf16[1,512,2048]{2,1,0:T(8,128)(2,1)S(1)}, bf16[1,512,2048]{2,1,0:T(8,128)(2,1)}, u32[]{:S(2)}) copy-start(bf16[1,512,2048]{2,1,0:T(8,128)(2,1)} %expand_ref.1) | copy-start | bytes 6291460
  2.0 2.9 %copy-start.4 = (bf16[1,2048,512]{2,1,0:T(8,128)(2,1)S(1)}, bf16[1,2048,512]{2,1,0:T(8,128)(2,1)}, u32[]{:S(2)}) copy-start(bf16[1,2048,512]{2,1,0:T(8,128)(2,1)} %contract_ref.1) | copy-start | bytes 6291460
  2.0 2.9 %copy-start.7 = (s32[1,3072]{1,0:T(1,128)S(1)}, s32[1,3072]{1,0:T(1,128)}, u32[]{:S(2)}) copy-start(s32[1,3072]{1,0:T(1,128)} %flags_ref.1) | copy-start | bytes 36868
  2.0 2.9 %copy-start.9 = (bf16[1,512]{1,0:T(2,128)(2,1)S(1)}, bf16[1,512]{1,0:T(2,128)(2,1)}, u32[]{:S(2)}) copy-start(bf16[1,512]{1,0:T(2,128)(2,1)} %readout_ref.1) | copy-start | bytes 3076
  2.1 2.9 %copy-start.11 = (f32[1,128]{1,0:T(1,128)S(1)}, f32[1,128]{1,0:T(1,128)}, u32[]{:S(2)}) copy-start(f32[1,128]{1,0:T(1,128)} %force_ref.1) | copy-start | bytes 1540
  7.3 4.5 %collective-permute-start.2 = (bf16[1,128]{1,0:T(2,128)(2,1)S(1)}, bf16[1,128]{1,0:T(2,128)(2,1)S(1)}, u32[]{:S(2)}, u32[]{:S(2)}) collective-permute-start(bf16[1,128]{1,0:T(2,128)(2,1)S(1)} %get-tuple-element.15), channel_id=1, source_target_pairs={{0,1},{2,3},{4,5},{6,7},{1,0},{3,2},{5,4},{7,6},{8,9},{10,11},{12,... | collective-permute-start | bytes 776 | tf_op jit(solution)/shard_map/ppermute | solution.py:377
  11.7 6.1 %collective-permute-start.5 = (bf16[2,128]{1,0:T(2,128)(2,1)S(1)}, bf16[2,128]{1,0:T(2,128)(2,1)S(1)}, u32[]{:S(2)}, u32[]{:S(2)}) collective-permute-start(bf16[2,128]{1,0:T(2,128)(2,1)S(1)} %pad_maximum_fusion.refs_0_), channel_id=1, source_target_pairs={{0,6},{1,7},{2,4},{3,5},{4,2},{5,3},{6,0},{7,1},{8,14},{9,15},{10,... | collective-permute-start | bytes 1544 | tf_op jit(solution)/shard_map/ppermute | solution.py:380
  16.3 4.4 %collective-permute-start.4 = (bf16[2,128]{1,0:T(2,128)(2,1)S(1)}, bf16[2,128]{1,0:T(2,128)(2,1)S(1)}, u32[]{:S(2)}, u32[]{:S(2)}) collective-permute-start(bf16[2,128]{1,0:T(2,128)(2,1)S(1)} %pad_maximum_fusion.refs_0_), channel_id=1, source_target_pairs={{0,4},{1,5},{2,6},{3,7},{4,0},{5,1},{6,2},{7,3},{8,12},{9,13},{10,... | collective-permute-start | bytes 1544 | tf_op jit(solution)/shard_map/ppermute | solution.py:380
  16.3 4.4 %collective-permute-start.3 = (bf16[2,128]{1,0:T(2,128)(2,1)S(1)}, bf16[2,128]{1,0:T(2,128)(2,1)S(1)}, u32[]{:S(2)}, u32[]{:S(2)}) collective-permute-start(bf16[2,128]{1,0:T(2,128)(2,1)S(1)} %pad_maximum_fusion.refs_0_), channel_id=1, source_target_pairs={{0,2},{1,3},{2,0},{3,1},{4,6},{5,7},{6,4},{7,5},{8,10},{9,11},{10,... | collective-permute-start | bytes 1544 | tf_op jit(solution)/shard_map/ppermute | solution.py:380
  16.9 3.8 %copy-start = (bf16[1,128,1024]{2,1,0:T(8,128)(2,1)S(1)}, bf16[1,128,1024]{2,1,0:T(8,128)(2,1)}, u32[]{:S(2)}) copy-start(bf16[1,128,1024]{2,1,0:T(8,128)(2,1)} %inverse_ref.1) | copy-start | bytes 786436
